TPU v7x, 256 devices: a whole 4x4x8 slice. The times are simulated.
256 devices in a mesh: row: 8 (over z), col: 16 (over x, y_lo, core), rep: 2 (over y_hi).
Axes of the slice: x: 4, y: 4 (y_hi: 2, y_lo: 2; y = y_hi * 2 + y_lo), z: 8, core: 2. Of those that a mesh axis runs over, the one named last changes fastest.
Arguments:
- a_blocks: bfloat16 [16384, 4096], P('row', 'col'), may hold values from -6 to 6
- a_mask: int32 [64, 16], P('row', 'col'), may hold values from 0 to 1, as said below
- b_blocks: bfloat16 [4096, 8192], P('row', 'col'), may hold values from -0.09375 to 0.09375
- b_mask: int32 [16, 32], P('row', 'col'), may hold values from 0 to 1
Outputs:
- c_product: bfloat16 [16384, 8192], P('row', ('col', 'rep'))
Inputs may be any that keep to these rules, and one draw needn't show every extreme that they name: a_mask holds 0 or 1; within each aligned tile of 8 block rows by 1 inner blocks (one device's tile) at most 2 entries are 1, and some tile holds exactly 2.
All inputs are finite; a program needn't handle non-finite values.
Results may differ from a plain program's by a relative error of at most 0.007.
Values may be sent and summed in bfloat16 or wider, within the bound.
A program may use at most 64 MiB of HBM per device.

v0:
```python
import jax
import jax.numpy as jnp
from jax import lax
from jax.sharding import PartitionSpec as P

BS = 256


def from_everyone(shard, axis):
    length = lax.axis_size(axis)
    return lax.all_to_all(
        jnp.broadcast_to(shard[None], (length, *shard.shape)), axis, 0, 0, tiled=True
    )


def in_order(pieces, dim):
    pieces = jnp.moveaxis(pieces, 0, dim)
    shape = pieces.shape
    return pieces.reshape(*shape[:dim], shape[dim] * shape[dim + 1], *shape[dim + 2 :])


def gather_directly(shard, axis, dim):
    pieces = from_everyone(shard, axis)
    return in_order(pieces, dim)


def expand(values, pattern):
    block_rows = pattern.shape[0]
    block_cols = pattern.shape[1]
    shaped = values.reshape(block_rows, BS, block_cols, BS) * pattern[:, None, :, None].astype(
        jnp.bfloat16
    )
    return shaped.reshape(block_rows * BS, block_cols * BS)


def pack_blocks(a_blocks, a_mask):
    block_rows = a_mask.shape[0]
    block_cols = a_mask.shape[1]
    slot_count = max(block_rows // 4, 1)
    flat_mask = a_mask.reshape(-1)
    slot_of = jnp.cumsum(flat_mask) - 1
    slot_ids = jnp.arange(slot_count, dtype=jnp.int32)[:, None]
    chosen = (flat_mask[None, :] == 1) & (slot_of[None, :] == slot_ids)
    flat_blocks = (
        a_blocks.reshape(block_rows, BS, block_cols, BS)
        .transpose(0, 2, 1, 3)
        .reshape(block_rows * block_cols, BS * BS)
    )
    packed = jnp.dot(
        chosen.astype(jnp.bfloat16), flat_blocks, preferred_element_type=jnp.float32
    ).astype(jnp.bfloat16)
    positions = jnp.arange(block_rows * block_cols, dtype=jnp.int32)
    chosen_int = chosen.astype(jnp.int32)
    used = jnp.sum(chosen_int, axis=1) > 0
    block_row = jnp.where(
        used, jnp.sum(chosen_int * (positions // block_cols)[None, :], axis=1), block_rows
    )
    block_inner = jnp.where(
        used, jnp.sum(chosen_int * (positions % block_cols)[None, :], axis=1), 0
    )
    codes = jnp.stack([block_row, block_inner], axis=1)
    return (packed.reshape(slot_count, BS, BS), codes)


def per_device(a_blocks, a_mask, b_blocks, b_mask):
    masked_b = expand(b_blocks, b_mask)
    layer_index = lax.axis_index("rep")
    c_width = masked_b.shape[1]
    own_width = c_width // 2
    own_b = lax.dynamic_slice_in_dim(masked_b, layer_index * own_width, own_width, 1)
    column_b = gather_directly(own_b, "row", 0)
    row_count = a_blocks.shape[0]
    block_rows = a_mask.shape[0]
    inner_local = a_mask.shape[1]
    inner_total = column_b.shape[0] // BS
    stacked_b = column_b.reshape(inner_total, BS, own_width)
    packed, codes = pack_blocks(a_blocks, a_mask)
    slot_count = packed.shape[0]
    row_ids = jnp.arange(block_rows, dtype=jnp.int32)
    blocks = lax.all_gather(packed, "col", axis=0, tiled=True)
    block_codes = lax.all_gather(codes, "col", axis=0, tiled=True)
    item_count = blocks.shape[0]
    owner = jnp.arange(item_count, dtype=jnp.int32) // slot_count
    inner = (owner * inner_local + block_codes[:, 1]).astype(jnp.int32)
    picked = jnp.take(stacked_b, inner, axis=0)
    partial_blocks = jnp.einsum("sij,sjn->sin", blocks, picked, preferred_element_type=jnp.float32)
    selector = (block_codes[:, 0][:, None] == row_ids[None, :]).astype(jnp.float32)
    summed = jnp.einsum("sr,sin->rin", selector, partial_blocks)
    product = summed.reshape(row_count, own_width)
    return product.astype(jnp.bfloat16)


def solution(mesh):
    in_specs = (P("row", "col"), P("row", "col"), P("row", "col"), P("row", "col"))
    out_specs = P("row", ("col", "rep"))
    return jax.shard_map(
        per_device, mesh=mesh, in_specs=in_specs, out_specs=out_specs, check_vma=False
    )
```

profile of v0, /device:TPU:4, one launch (start us, length us, event | category | flops | bytes accessed | tf_op | source)
XLA Modules:
  0.0 90.8 jit_solution(8333974112397646809)
XLA Ops:
  6.5 0.0 copy-start.1
  6.5 0.0 copy-start
  6.5 0.0 all-gather.3.cloned.1.call-start
  6.5 0.7 compare_bitcast_fusion
  7.3 0.8 reduce-window.8
  8.1 1.7 %reshape_transpose_reshape.3 = bf16[8,65536]{1,0:T(8,128)(2,1)S(1)} reshape(bf16[2048,256]{1,0:T(8,128)(2,1)} %param.4) | data formatting | bytes 2097152 | tf_op jit(solution)/shard_map/reshape;transpose;reshape | solution.py:47
  9.8 0.1 convert_reduce_fusion
  9.9 0.4 convolution_convert_fusion
  10.4 0.7 copy.29
  11.1 0.0 all-gather.3.cloned.1.call-update
  11.1 0.0 copy-done.1
  11.2 0.3 mul.31
  11.5 0.1 copy.23
  11.6 0.0 copy-done
  11.6 0.1 dynamic-slice_multiply_fusion
  11.7 1.5 %broadcast_in_dim.29 = bf16[8,512,256]{2,1,0:T(8,128)(2,1)} broadcast(bf16[512,256]{1,0:T(8,128)(2,1)S(1)} %dynamic-slice_multiply_fusion), dimensions={1,2} | broadcast | bytes 2359296 | tf_op jit(solution)/shard_map/broadcast_in_dim | solution.py:12
  13.2 8.5 %all-to-all-start = ((bf16[8,512,256]{2,1,0:T(8,128)(2,1)}), bf16[8,512,256]{2,1,0:T(8,128)(2,1)S(1)}, u32[]{:S(2)}, u32[]{:S(2)}) async-start(bf16[8,512,256]{2,1,0:T(8,128)(2,1)} %broadcast_in_dim.29), calls=%async_computation | async-start | bytes 4194304 | tf_op jit(solution)/shard_map/all_to_all | solution.py:11
  21.6 0.1 copy.21
  21.7 15.4 %all-gather = s32[16,2,2]{2,1,0:T(2,128)S(1)} all-gather(s32[1,2,2]{2,1,0:T(2,128)S(1)} %pad_bitcast_fusion), channel_id=1, replica_groups=mesh['row'=8,'col'=16,'rep'=2] {'col'}, dimensions={0}, use_global_device_ids=true | all-gather | bytes 272 | tf_op jit(solution)/shard_map/all_gather | solution.py:81
  37.1 0.1 fusion.15
  37.2 0.1 copy.19
  37.3 0.1 copy.20
  37.4 35.4 %all-to-all-done = bf16[8,512,256]{2,1,0:T(8,128)(2,1)S(1)} async-done(((bf16[8,512,256]{2,1,0:T(8,128)(2,1)}), bf16[8,512,256]{2,1,0:T(8,128)(2,1)S(1)}, u32[]{:S(2)}, u32[]{:S(2)}) %all-to-all-start) | async-done | bytes 2097184 | tf_op jit(solution)/shard_map/all_to_all | solution.py:11
  72.8 2.8 %gather_fusion = bf16[32,256,256]{2,1,0:T(8,128)(2,1)} fusion(bf16[16,256,256]{2,1,0:T(8,128)(2,1)S(1)} %bitcast.28, s32[1024]{0:T(1024)S(1)} %pad_clamp_fusion), kind=kCustom, calls=%fused_computation | custom fusion | bytes 8388736 | tf_op jit(solution)/shard_map/jit(_take)/gather | solution.py:85
  75.6 0.0 all-gather.3.cloned.1.call-done
  75.6 4.8 %fusion.2 = bf16[32,256,256]{2,1,0:T(8,128)(2,1)S(1)} fusion(bf16[32,256,256]{2,1,0:T(8,128)(2,1)} %all-gather.3.cloned.1.call-done, bf16[32,256,256]{2,1,0:T(8,128)(2,1)} %gather_fusion, pred[32]{0:T(512)(128)(4,1)S(1)} %get-tuple-element.7), kind=kOutput, calls=%fused_computation.4 | convolution fusion | flops 1075838976 | bytes 12582944 | tf_op jit(solution)/shard_map/sij,sjn->sin/dot_general | solution.py:86
  80.4 2.4 %fusion.6 = bf16[8,256,256]{2,0,1:T(8,128)(2,1)S(1)} fusion(bf16[32,256,256]{2,1,0:T(8,128)(2,1)S(1)} %fusion.2, s32[32]{0:T(128)S(1)} %bitcast.34), kind=kOutput, calls=%fused_computation.8 | convolution fusion | flops 33554688 | bytes 5243008 | tf_op jit(solution)/shard_map/sr,sin->rin/dot_general | solution.py:88
  82.8 1.2 %copy.17 = bf16[8,256,256]{2,1,0:T(8,128)(2,1)} copy(bf16[8,256,256]{2,0,1:T(8,128)(2,1)S(1)} %fusion.6) | data formatting | bytes 2097152 | tf_op jit(solution)/shard_map/convert_element_type | solution.py:90
  (6 shorter events, 0.0 us)
Async XLA Ops:
  6.5 4.6 %copy-start.1 = (s32[2,2]{1,0:T(2,128)S(1)}, s32[2,2]{1,0:T(2,128)}, u32[]{:S(2)}) copy-start(s32[2,2]{1,0:T(2,128)} %param.7) | copy-start | bytes 52
  6.5 5.1 %copy-start = (bf16[512,512]{1,0:T(8,128)(2,1)S(1)}, bf16[512,512]{1,0:T(8,128)(2,1)}, u32[]{:S(2)}) copy-start(bf16[512,512]{1,0:T(8,128)(2,1)} %param.6) | copy-start | bytes 1572868
  6.5 69.1 %all-gather.3.cloned.1.call-start = ((), (), s32[]{:S(2)}) async-start(), calls=%async_computation.1 | async-start | bytes 4456448 | tf_op jit(solution)/shard_map/all_gather | solution.py:80
  13.2 59.7 %all-to-all-start = ((bf16[8,512,256]{2,1,0:T(8,128)(2,1)}), bf16[8,512,256]{2,1,0:T(8,128)(2,1)S(1)}, u32[]{:S(2)}, u32[]{:S(2)}) async-start(bf16[8,512,256]{2,1,0:T(8,128)(2,1)} %broadcast_in_dim.29), calls=%async_computation | async-start | bytes 4194304 | tf_op jit(solution)/shard_map/all_to_all | solution.py:11
Sparse Core Ops, SparseCore 0:
  11.3 41.8 all-gather.2
where the time goes:
time: 91 us; the launch traced here: 90.8 us
  waiting for transfers between devices  35.4 us (39%)
  blocking collectives  15.4 us (17%)
  between operations  13.5 us (15%)
  local copies, waits for them, and re-layouts  8.6 us (9%)
  starting transfers between devices  8.47 us (9%)
  matrix products  7.58 us (8%)
  other arithmetic  1.81 us (2%)
    all_to_all x1, waiting for transfers between devices, from_everyone(): lax.all_to_all(jnp.broadcast_to(shard[None], (length, *shard.shape)), axi...  35.4 us
    all_gather x1, blocking collectives, per_device(): block_codes = lax.all_gather(codes, 'col', axis=0, tiled=True)  15.4 us
    all_to_all x1, starting transfers between devices, from_everyone(): lax.all_to_all(jnp.broadcast_to(shard[None], (length, *shard.shape)), axi...  8.47 us
    dot_general x1, matrix products, per_device(): jnp.einsum('sij,sjn->sin', blocks, picked, preferred_element_type=jnp.flo...  4.8 us
    gather x1, local copies, waits for them, and re-layouts, per_device(): picked = jnp.take(stacked_b, inner, axis=0)  2.77 us
    dot_general x1, matrix products, per_device(): summed = jnp.einsum('sr,sin->rin', selector, partial_blocks)  2.35 us
  transfers between devices with their start and end apart: 2, of which 1 were waited for; matrix products, arithmetic and copies ran while one was open for 6% of the time, Pallas kernels for 0%

commit v1 on v0

--- a/solution.py
+++ b/solution.py
@@ -78,7 +78,9 @@
     slot_count = packed.shape[0]
     row_ids = jnp.arange(block_rows, dtype=jnp.int32)
     blocks = lax.all_gather(packed, "col", axis=0, tiled=True)
-    block_codes = lax.all_gather(codes, "col", axis=0, tiled=True)
+    block_codes = jnp.concatenate(
+        lax.all_to_all(jnp.stack([codes] * lax.axis_size("col")), "col", 0, 0), axis=0
+    )
     item_count = blocks.shape[0]
     owner = jnp.arange(item_count, dtype=jnp.int32) // slot_count
     inner = (owner * inner_local + block_codes[:, 1]).astype(jnp.int32)

time: 91 us -> 103 us (1.13); the launches traced: 90.8 us -> 101 us
  waiting for transfers between devices: 35.4 us -> 54.6 us
  blocking collectives: 15.4 us -> 0 us
  starting transfers between devices: 8.47 us -> 14.3 us
    all_to_all x1, waiting for transfers between devices: 35.4 us -> 51.3 us  [from_everyone(): lax.all_to_all(jnp.broadcast_to(shard[None], (length, *shard.shape)), axi...]
    all_gather x1 -> x0, blocking collectives: 15.4 us -> none  [per_device(): block_codes = lax.all_gather(codes, 'col', axis=0, tiled=True)]
    all_to_all x0 -> x1, starting transfers between devices: none -> 5.84 us  [per_device(): lax.all_to_all(jnp.stack([codes] * lax.axis_size('col')), 'col', 0, 0)]
    all_to_all x0 -> x1, waiting for transfers between devices: none -> 3.29 us  [per_device(): lax.all_to_all(jnp.stack([codes] * lax.axis_size('col')), 'col', 0, 0)]
  transfers between devices with their start and end apart: 2 -> 3, of which waited for: 1 -> 2; matrix products, arithmetic and copies ran while one was open for 6% -> 5% of each run, Pallas kernels for 0% -> 0%
where the time goes in v1:
time: 103 us; the launch traced here: 101 us
  waiting for transfers between devices  54.6 us (53%)
  starting transfers between devices  14.3 us (14%)
  between operations  13.5 us (13%)
  local copies, waits for them, and re-layouts  8.98 us (9%)
  matrix products  7.58 us (7%)
  other arithmetic  1.81 us (2%)
    all_to_all x1, waiting for transfers between devices, from_everyone(): lax.all_to_all(jnp.broadcast_to(shard[None], (length, *shard.shape)), axi...  51.3 us
    all_to_all x1, starting transfers between devices, from_everyone(): lax.all_to_all(jnp.broadcast_to(shard[None], (length, *shard.shape)), axi...  8.47 us
    all_to_all x1, starting transfers between devices, per_device(): lax.all_to_all(jnp.stack([codes] * lax.axis_size('col')), 'col', 0, 0)  5.84 us
    dot_general x1, matrix products, per_device(): jnp.einsum('sij,sjn->sin', blocks, picked, preferred_element_type=jnp.flo...  4.8 us
    all_to_all x1, waiting for transfers between devices, per_device(): lax.all_to_all(jnp.stack([codes] * lax.axis_size('col')), 'col', 0, 0)  3.29 us
    gather x1, local copies, waits for them, and re-layouts, per_device(): picked = jnp.take(stacked_b, inner, axis=0)  2.79 us
    dot_general x1, matrix products, per_device(): summed = jnp.einsum('sr,sin->rin', selector, partial_blocks)  2.35 us
  transfers between devices with their start and end apart: 3, of which 2 were waited for; matrix products, arithmetic and copies ran while one was open for 5% of the time, Pallas kernels for 0%

profile of v1, /device:TPU:4, one launch (start us, length us, event | category | flops | bytes accessed | tf_op | source)
XLA Modules:
  0.0 100.8 jit_solution(3396335847836139862)
XLA Ops:
  6.5 0.0 copy-start.1
  6.5 0.0 copy-start
  6.5 0.0 all-gather.2.cloned.1.call-start
  6.5 0.7 compare_bitcast_fusion
  7.3 0.8 reduce-window.8
  8.1 1.7 %reshape_transpose_reshape.3 = bf16[8,65536]{1,0:T(8,128)(2,1)S(1)} reshape(bf16[2048,256]{1,0:T(8,128)(2,1)} %param.4) | data formatting | bytes 2097152 | tf_op jit(solution)/shard_map/reshape;transpose;reshape | solution.py:47
  9.8 0.1 convert_reduce_fusion
  9.9 0.4 convolution_convert_fusion
  10.4 0.7 copy.19
  11.1 0.0 all-gather.2.cloned.1.call-update
  11.2 0.6 stack.5
  11.8 5.8 %all-to-all-start = ((s32[16,2,2]{1,2,0:T(2,128)}), s32[16,2,2]{1,2,0:T(2,128)S(1)}, u32[]{:S(2)}, u32[]{:S(2)}) async-start(s32[16,2,2]{1,2,0:T(2,128)} %stack.5), calls=%async_computation | async-start | bytes 32768 | tf_op jit(solution)/shard_map/all_to_all | solution.py:82
  17.6 0.0 copy-done.1
  17.6 0.3 mul.31
  18.0 0.1 copy.13
  18.1 0.0 copy-done
  18.1 0.1 dynamic-slice_multiply_fusion
  18.2 3.3 %all-to-all-done = s32[16,2,2]{1,2,0:T(2,128)S(1)} async-done(((s32[16,2,2]{1,2,0:T(2,128)}), s32[16,2,2]{1,2,0:T(2,128)S(1)}, u32[]{:S(2)}, u32[]{:S(2)}) %all-to-all-start) | async-done | bytes 288 | tf_op jit(solution)/shard_map/all_to_all | solution.py:82
  21.4 1.5 %broadcast_in_dim.29 = bf16[8,512,256]{2,1,0:T(8,128)(2,1)} broadcast(bf16[512,256]{1,0:T(8,128)(2,1)S(1)} %dynamic-slice_multiply_fusion), dimensions={1,2} | broadcast | bytes 2359296 | tf_op jit(solution)/shard_map/broadcast_in_dim | solution.py:12
  22.9 8.5 %all-to-all-start.1 = ((bf16[8,512,256]{2,1,0:T(8,128)(2,1)}), bf16[8,512,256]{2,1,0:T(8,128)(2,1)S(1)}, u32[]{:S(2)}, u32[]{:S(2)}) async-start(bf16[8,512,256]{2,1,0:T(8,128)(2,1)} %broadcast_in_dim.29), calls=%async_computation.1 | async-start | bytes 4194304 | tf_op jit(solution)/shard_map/all_to_all | solution.py:11
  31.4 0.1 reshape.111
  31.5 51.3 %all-to-all-done.1 = bf16[8,512,256]{2,1,0:T(8,128)(2,1)S(1)} async-done(((bf16[8,512,256]{2,1,0:T(8,128)(2,1)}), bf16[8,512,256]{2,1,0:T(8,128)(2,1)S(1)}, u32[]{:S(2)}, u32[]{:S(2)}) %all-to-all-start.1) | async-done | bytes 2097184 | tf_op jit(solution)/shard_map/all_to_all | solution.py:11
  82.8 2.8 %gather_fusion = bf16[32,256,256]{2,1,0:T(8,128)(2,1)} fusion(bf16[16,256,256]{2,1,0:T(8,128)(2,1)S(1)} %bitcast.28, s32[1024]{0:T(1024)S(1)} %pad_clamp_fusion), kind=kCustom, calls=%fused_computation | custom fusion | bytes 8388736 | tf_op jit(solution)/shard_map/jit(_take)/gather | solution.py:87
  85.6 0.0 all-gather.2.cloned.1.call-done
  85.6 4.8 %fusion.2 = bf16[32,256,256]{2,1,0:T(8,128)(2,1)S(1)} fusion(bf16[32,256,256]{2,1,0:T(8,128)(2,1)} %all-gather.2.cloned.1.call-done, bf16[32,256,256]{2,1,0:T(8,128)(2,1)} %gather_fusion, pred[32]{0:T(512)(128)(4,1)S(1)} %get-tuple-element.7), kind=kOutput, calls=%fused_computation.4 | convolution fusion | flops 1075838976 | bytes 12582944 | tf_op jit(solution)/shard_map/sij,sjn->sin/dot_general | solution.py:88
  90.4 2.4 %fusion.6 = bf16[8,256,256]{2,0,1:T(8,128)(2,1)S(1)} fusion(bf16[32,256,256]{2,1,0:T(8,128)(2,1)S(1)} %fusion.2, s32[32]{0:T(128)S(1)} %slice_bitcast_fusion), kind=kOutput, calls=%fused_computation.8 | convolution fusion | flops 33554688 | bytes 5243008 | tf_op jit(solution)/shard_map/sr,sin->rin/dot_general | solution.py:90
  92.8 1.2 %copy.11 = bf16[8,256,256]{2,1,0:T(8,128)(2,1)} copy(bf16[8,256,256]{2,0,1:T(8,128)(2,1)S(1)} %fusion.6) | data formatting | bytes 2097152 | tf_op jit(solution)/shard_map/convert_element_type | solution.py:92
  (8 shorter events, 0.0 us)
Async XLA Ops:
  6.5 11.1 %copy-start.1 = (s32[2,2]{1,0:T(2,128)S(1)}, s32[2,2]{1,0:T(2,128)}, u32[]{:S(2)}) copy-start(s32[2,2]{1,0:T(2,128)} %param.7) | copy-start | bytes 52
  6.5 11.5 %copy-start = (bf16[512,512]{1,0:T(8,128)(2,1)S(1)}, bf16[512,512]{1,0:T(8,128)(2,1)}, u32[]{:S(2)}) copy-start(bf16[512,512]{1,0:T(8,128)(2,1)} %param.6) | copy-start | bytes 1572868
  6.5 79.1 %all-gather.2.cloned.1.call-start = ((), (), s32[]{:S(2)}) async-start(), calls=%async_computation.2 | async-start | bytes 4456448 | tf_op jit(solution)/shard_map/all_gather | solution.py:80
  11.8 9.7 %all-to-all-start = ((s32[16,2,2]{1,2,0:T(2,128)}), s32[16,2,2]{1,2,0:T(2,128)S(1)}, u32[]{:S(2)}, u32[]{:S(2)}) async-start(s32[16,2,2]{1,2,0:T(2,128)} %stack.5), calls=%async_computation | async-start | bytes 32768 | tf_op jit(solution)/shard_map/all_to_all | solution.py:82
  22.9 59.9 %all-to-all-start.1 = ((bf16[8,512,256]{2,1,0:T(8,128)(2,1)}), bf16[8,512,256]{2,1,0:T(8,128)(2,1)S(1)}, u32[]{:S(2)}, u32[]{:S(2)}) async-start(bf16[8,512,256]{2,1,0:T(8,128)(2,1)} %broadcast_in_dim.29), calls=%async_computation.1 | async-start | bytes 4194304 | tf_op jit(solution)/shard_map/all_to_all | solution.py:11
Sparse Core Ops, SparseCore 0:
  11.3 41.8 all-gather.1
